TPU v7x, 256 devices: a whole 4x4x8 slice. The times are simulated.
256 devices in a mesh: group: 16 (over y, x), ingroup: 16 (over z, core).
Axes of the slice: x: 4, y: 4, z: 8, core: 2. Of those that a mesh axis runs over, the one named last changes fastest.
Arguments:
- activations: bfloat16 [16384, 3584], P(('group', 'ingroup')), may hold values from -6 to 6
- gate_weights: bfloat16 [256, 1792, 1024], P(('group', 'ingroup')), may hold values from -0.09375 to 0.09375
- up_weights: bfloat16 [256, 1792, 1024], P(('group', 'ingroup')), may hold values from -0.09375 to 0.09375
- down_weights: bfloat16 [256, 1024, 1792], P(('group', 'ingroup')), may hold values from -0.375 to 0.375
- expert_ids: int32 [16384, 8], P(('group', 'ingroup')), may hold values from 0 to 127, as said below
- gate_scores: int32 [16384, 8], P(('group', 'ingroup')), may hold values from 1 to 15
- arrival_pos: int32 [16384], P(('group', 'ingroup')), may hold values from 0 to 63, as said below
Outputs:
- expert_mix: bfloat16 [16384, 3584], P(('group', 'ingroup'))
Inputs may be any that keep to these rules, and one draw needn't show every extreme that they name: `expert_ids`: each row names 8 different experts, two from each of 4 different groups. Among one device's 64 rows no expert is named more than 6 times and no group by more than 24 rows; on every device some expert is named exactly 6 times and some group by exactly 24 rows. `arrival_pos`: within each device's 64 rows the values are a permutation.
All inputs are finite; a program needn't handle non-finite values.
Results may differ from a plain program's by a relative error of at most 0.0077.
Values may be sent and summed in bfloat16 or wider, within the bound.
No kernel may reach another device: no remote copies, remote signals or barrier semaphores. Data moves between devices by JAX's collectives and lax.ppermute only.
A program may use at most 128 MiB of HBM per device.

v0:
```python
import jax
import jax.numpy as jnp
from jax import lax
from jax.sharding import PartitionSpec as P

TOPG = 4


def from_partner(shard, axis, apart):
    return lax.ppermute(shard, axis, [(i, i ^ 1 << apart) for i in range(lax.axis_size(axis))])


def group_layout(int_table, groups, members, expert_most):
    shaped = int_table.reshape(groups, members // 2, 1, expert_most)
    shaped = jnp.broadcast_to(shaped, (groups, members // 2, 2, expert_most))
    return shaped.reshape(groups, members, expert_most)


def per_device(
    activations, gate_weights, up_weights, down_weights, expert_ids, gate_scores, arrival_pos
):
    groups = lax.axis_size("group")
    members = lax.axis_size("ingroup")
    per_group = members // 2
    experts = groups * per_group
    tok_count = activations.shape[0]
    model_width = activations.shape[1]
    half_width = model_width // 2
    top_picks = expert_ids.shape[1]
    capacity = 2 * top_picks * tok_count
    group_most = min(tok_count, 3 * tok_count * TOPG // (2 * groups))
    expert_most = (2 * group_most + per_group - 1) // per_group
    expert_range = jnp.arange(experts, dtype=jnp.int32)
    pick_hits = (expert_ids[:, :, None] == expert_range[None, None, :]).astype(jnp.int32)
    hit_table = jnp.sum(pick_hits, axis=1)
    occurrence = jnp.cumsum(hit_table, axis=0) - hit_table
    position_range = jnp.arange(tok_count, dtype=jnp.int32)
    arrival_table = (arrival_pos[:, None] == position_range[None, :]).astype(jnp.int32)
    own_counts = jnp.dot(hit_table.T, arrival_table)
    shifts = jnp.arange(32, dtype=jnp.int32)
    flat_bits = own_counts.reshape(-1, 32)
    packed = jnp.sum(jnp.left_shift(flat_bits, shifts[None, :]), axis=1)[None, :]
    my_index = lax.axis_index(("group", "ingroup"))
    piece = lax.all_gather(packed, ("group", "ingroup"), axis=0, tiled=True)
    bit_table = jnp.bitwise_and(jnp.right_shift(piece[:, :, None], shifts[None, None, :]), 1)
    bit_table = bit_table.reshape(piece.shape[0], experts, tok_count)
    source_index = jnp.arange(piece.shape[0], dtype=jnp.int32)
    earlier_flag = (source_index < my_index).astype(jnp.int32)
    prior_part = jnp.sum(bit_table * earlier_flag[:, None, None], axis=0)
    total_part = jnp.sum(bit_table, axis=0)
    earlier = jnp.cumsum(total_part, axis=1) - total_part
    rank_table = earlier + prior_part
    rank_by_token = jnp.dot(arrival_table, rank_table.T)
    pick_rank = jnp.sum(pick_hits * rank_by_token[:, None, :], axis=2)
    pick_occurrence = jnp.sum(pick_hits * occurrence[:, None, :], axis=2)
    kept_mask = (pick_rank < capacity).astype(jnp.int32)
    kept_scores = gate_scores * kept_mask
    weight_sum = jnp.maximum(jnp.sum(kept_scores, axis=1), 1)
    routing = kept_scores.astype(jnp.float32) / weight_sum.astype(jnp.float32)[:, None]
    slot_range = jnp.arange(expert_most, dtype=jnp.int32)
    slot_match = hit_table[:, :, None] * (
        occurrence[:, :, None] == slot_range[None, None, :]
    ).astype(jnp.int32)
    slot_valid = jnp.sum(slot_match, axis=0)
    slot_token = jnp.sum(slot_match * position_range[:, None, None], axis=0)
    slot_rank = jnp.sum(slot_match * rank_by_token[:, :, None], axis=0)
    send_rank = jnp.where((slot_valid > 0) & (slot_rank < capacity), slot_rank, -1)
    half_index = jnp.arange(members, dtype=jnp.int32) % 2
    token_layout = jnp.transpose(group_layout(slot_token, groups, members, expert_most), (1, 0, 2))
    rank_layout = jnp.transpose(group_layout(send_rank, groups, members, expert_most), (1, 0, 2))
    feature_rows = activations.reshape(tok_count * 2, half_width)
    send_rows = jnp.take(feature_rows, token_layout * 2 + half_index[:, None, None], axis=0)
    got_rows, got_rank = (
        lax.all_to_all(
            lax.all_to_all(send_rows, "group", split_axis=1, concat_axis=1, tiled=True),
            "ingroup",
            split_axis=0,
            concat_axis=0,
            tiled=True,
        ),
        lax.all_to_all(
            lax.all_to_all(rank_layout, "group", split_axis=1, concat_axis=1, tiled=True),
            "ingroup",
            split_axis=0,
            concat_axis=0,
            tiled=True,
        ),
    )
    slot_total = members * groups * expert_most
    flat_rank = got_rank.reshape(slot_total)
    flat_rows = got_rows.reshape(slot_total, half_width)
    target = jnp.where(flat_rank >= 0, flat_rank, capacity)
    source_of = (
        jnp.zeros((capacity,), jnp.int32)
        .at[target]
        .set(jnp.arange(slot_total, dtype=jnp.int32), mode="drop")
    )
    filled = jnp.zeros((capacity,), jnp.bool_).at[target].set(True, mode="drop")
    expert_rows = jnp.where(
        filled[:, None], jnp.take(flat_rows, source_of, axis=0), jnp.zeros((), activations.dtype)
    )
    gate_part = jnp.dot(expert_rows, gate_weights[0], preferred_element_type=jnp.float32).astype(
        jnp.bfloat16
    )
    up_part = jnp.dot(expert_rows, up_weights[0], preferred_element_type=jnp.float32).astype(
        jnp.bfloat16
    )
    other_gate, other_up = from_partner((gate_part, up_part), "ingroup", 0)
    gate_sum = gate_part.astype(jnp.float32) + other_gate.astype(jnp.float32)
    up_sum = up_part.astype(jnp.float32) + other_up.astype(jnp.float32)
    hidden = (jax.nn.silu(gate_sum) * up_sum).astype(jnp.bfloat16)
    expert_out = jnp.dot(hidden, down_weights[0], preferred_element_type=jnp.float32).astype(
        jnp.bfloat16
    )
    back_rows = jnp.take(expert_out, jnp.clip(flat_rank, 0, capacity - 1), axis=0)
    back_rows = jnp.where((flat_rank >= 0)[:, None], back_rows, jnp.zeros((), jnp.bfloat16))
    back_rows = back_rows.reshape(members, groups, expert_most, half_width)
    pick_group = expert_ids // per_group
    returned = lax.all_to_all(
        lax.all_to_all(back_rows, "group", split_axis=1, concat_axis=1, tiled=True),
        "ingroup",
        split_axis=0,
        concat_axis=0,
        tiled=True,
    )
    pick_member = expert_ids % per_group * 2
    halves = jnp.arange(2, dtype=jnp.int32)
    flat_pick = (
        (pick_member[:, :, None] + halves[None, None, :]) * groups + pick_group[:, :, None]
    ) * expert_most + pick_occurrence[:, :, None]
    gathered = jnp.take(returned.reshape(slot_total, half_width), flat_pick, axis=0)
    terms = routing[:, :, None] * gathered.reshape(tok_count, top_picks, model_width).astype(
        jnp.float32
    )
    pick_range = jnp.arange(top_picks, dtype=jnp.int32)
    not_self = (pick_range[:, None] != pick_range[None, :]).astype(jnp.int32)
    same_other = (pick_group[:, :, None] == pick_group[:, None, :]).astype(jnp.int32) * not_self[
        None, :, :
    ]
    partner = jnp.sum(same_other * pick_range[None, None, :], axis=2)
    partner_terms = jnp.take_along_axis(terms, partner[:, :, None], axis=1)
    paired = terms + partner_terms
    rounded = lax.optimization_barrier(paired.astype(jnp.bfloat16)).astype(jnp.float32)
    combined = 0.5 * jnp.sum(rounded, axis=1)
    return combined.astype(jnp.bfloat16)


def solution(mesh):
    return jax.shard_map(
        per_device,
        mesh=mesh,
        in_specs=(
            P(("group", "ingroup"), None),
            P(("group", "ingroup"), None, None),
            P(("group", "ingroup"), None, None),
            P(("group", "ingroup"), None, None),
            P(("group", "ingroup"), None),
            P(("group", "ingroup"), None),
            P(("group", "ingroup")),
        ),
        out_specs=P(("group", "ingroup"), None),
        check_vma=False,
    )
```

profile of v0, /device:TPU:1, one launch (start us, length us, event | category | flops | bytes accessed | tf_op | source)
XLA Modules:
  0.0 716.8 jit_solution(8007721992500397717)
XLA Ops:
  0.0 0.8 copy.125
  0.8 0.1 convert_reduce_fusion.1
  1.0 0.9 fusion.22
  2.0 0.1 shift-left_reduce_fusion
  2.1 67.0 %all-gather.1 = s32[256,1,256]{2,1,0:T(1,128)S(1)} all-gather(s32[1,1,256]{2,1,0:T(1,128)S(1)} %bitcast.53), channel_id=2, replica_groups=mesh['group'=16,'ingroup'=16] {'group','ingroup'}, dimensions={0}, use_global_device_ids=true | all-gather | bytes 263168 | tf_op jit(solution)/shard_map/all_gather | solution.py:44
  69.2 1.7 fusion
  71.2 0.1 reduce_window_sum.23
  71.7 0.9 fusion.19
  72.9 0.7 copy.142
  73.7 4.2 all-to-all-start
  78.3 0.2 copy.149
  78.4 0.1 reshape.254
  78.6 0.2 reshape.248
  78.8 6.7 gather_fusion
  85.5 9.6 %reshape.253 = bf16[16,16,6,1792]{3,2,1,0:T(8,128)(2,1)} reshape(bf16[1536,1792]{1,0:T(8,128)(2,1)} %gather_fusion) | data formatting | bytes 11010048 | tf_op jit(solution)/shard_map/jit(_take)/gather | solution.py:72
  95.1 0.2 copy.148
  95.3 4.0 broadcast_select_fusion
  99.3 5.5 copy.150
  104.8 6.7 all-to-all-start.2
  111.5 0.7 copy.143
  112.2 80.3 %all-to-all-done.2 = bf16[16,16,6,1792]{3,0,2,1:T(8,128)(2,1)} async-done(((bf16[16,16,6,1792]{3,0,2,1:T(8,128)(2,1)}), bf16[16,16,6,1792]{3,0,2,1:T(8,128)(2,1)}, u32[]{:S(2)}, u32[]{:S(2)}) %all-to-all-start.2) | async-done | bytes 5505056 | tf_op jit(solution)/shard_map/all_to_all | solution.py:75
  192.5 6.3 all-to-all-start.1
  198.8 7.9 %copy.151 = bf16[16,16,6,1792]{3,1,2,0:T(8,128)(2,1)} copy(bf16[16,16,6,1792]{3,0,2,1:T(8,128)(2,1)} %all-to-all-done.2) | data formatting | bytes 11010048 | tf_op jit(solution)/shard_map/all_to_all | solution.py:75
  206.7 7.2 %all-to-all-start.3 = ((bf16[16,16,6,1792]{3,1,2,0:T(8,128)(2,1)}), bf16[16,16,6,1792]{3,1,2,0:T(8,128)(2,1)}, u32[]{:S(2)}, u32[]{:S(2)}) async-start(bf16[16,16,6,1792]{3,1,2,0:T(8,128)(2,1)} %copy.151), calls=%async_computation.3 | async-start | bytes 11010048 | tf_op jit(solution)/shard_map/all_to_all | solution.py:74
  213.9 0.2 copy.146
  214.1 0.1 reshape.247
  214.3 6.2 scatter_custom_fusion.1
  220.5 11.6 %scatter_custom_fusion = pred[1024]{0:T(1024)(128)(4,1)S(1)} fusion(s32[1536]{0:T(1024)S(1)} %get-tuple-element.13, pred[1536]{0:T(1024)(128)(4,1)S(1)} %broadcast.331, pred[]{:T(512)} %constant.148.clone.1), kind=kCustom, calls=%fused_computation.100 | custom fusion | bytes 1025 | tf_op jit(solution)/shard_map/scatter | solution.py:98
  232.2 103.5 %all-to-all-done.3 = bf16[16,16,6,1792]{3,1,2,0:T(8,128)(2,1)} async-done(((bf16[16,16,6,1792]{3,1,2,0:T(8,128)(2,1)}), bf16[16,16,6,1792]{3,1,2,0:T(8,128)(2,1)}, u32[]{:S(2)}, u32[]{:S(2)}) %all-to-all-start.3) | async-done | bytes 5505056 | tf_op jit(solution)/shard_map/all_to_all | solution.py:74
  335.7 7.7 %copy.152 = bf16[16,16,6,1792]{3,2,1,0:T(8,128)(2,1)} copy(bf16[16,16,6,1792]{3,1,2,0:T(8,128)(2,1)} %all-to-all-done.3) | data formatting | bytes 11010048 | tf_op jit(solution)/shard_map/all_to_all | solution.py:74
  343.3 9.7 %reshape.249 = bf16[1536,1792]{1,0:T(8,128)(2,1)} reshape(bf16[16,16,6,1792]{3,2,1,0:T(8,128)(2,1)} %copy.152) | data formatting | bytes 11010048 | tf_op jit(solution)/shard_map/reshape | solution.py:91
  353.0 11.2 %gather_fusion.1 = bf16[1024,1792]{1,0:T(8,128)(2,1)} fusion(bf16[1536,1792]{1,0:T(8,128)(2,1)} %reshape.249, s32[1024]{0:T(1024)S(1)} %fusion.37), kind=kCustom, calls=%fused_computation.1 | custom fusion | bytes 7344128 | tf_op jit(solution)/shard_map/jit(_take)/gather | solution.py:100
  364.2 7.3 %fusion.10 = bf16[1024,1024]{1,0:T(8,128)(2,1)S(1)} fusion(bf16[1,1792,1024]{2,1,0:T(8,128)(2,1)} %param.8, bf16[1024,1792]{1,0:T(8,128)(2,1)} %gather_fusion.1, pred[1024]{0:T(1024)(128)(4,1)S(1)} %compare_and_fusion.3, pred[1024]{0:T(1024)(128)(4,1)S(1)} %scatter_custom_fusion), kind=kOutput, calls=%fused_computation.28 | convolution fusion | flops 3762814976 | bytes 9439232 | tf_op jit(solution)/shard_map/dot_general | solution.py:102
  371.5 1.0 collective-permute-start
  372.5 5.6 fusion.13
  378.1 0.2 collective-permute-start.1
  378.3 0.2 copy.144
  378.5 0.2 copy.145
  378.7 4.0 collective-permute-done.1
  382.7 10.9 %convolution_convert_fusion = bf16[1024,1792]{1,0:T(8,128)(2,1)} fusion(bf16[1,1024,1792]{2,1,0:T(8,128)(2,1)} %param.10, bf16[1024,1024]{1,0:T(8,128)(2,1)} %collective-permute-done.1, bf16[1024,1024]{1,0:T(8,128)(2,1)} %fusion.13, bf16[1024,1024]{1,0:T(8,128)(2,1)} %collective-permute-done, bf16[1024,1024]{1,0:T(8,128)(2,1)S(1)} %fusion.10), kind=kOutput, calls=%fused_computation.18 | convolution fusion | flops 3772514304 | bytes 15728640 | tf_op jit(solution)/shard_map/dot_general | solution.py:112
  393.6 13.9 %gather_fusion.2 = bf16[1536,1792]{1,0:T(8,128)(2,1)} fusion(bf16[1024,1792]{1,0:T(8,128)(2,1)} %convolution_convert_fusion, s32[2048]{0:T(1024)S(1)} %pad_clamp_fusion), kind=kCustom, calls=%fused_computation.2 | custom fusion | bytes 11016192 | tf_op jit(solution)/shard_map/jit(_take)/gather | solution.py:115
  407.5 9.6 %gather.25 = bf16[16,16,6,1792]{3,2,1,0:T(8,128)(2,1)} reshape(bf16[1536,1792]{1,0:T(8,128)(2,1)} %gather_fusion.2) | data formatting | bytes 11010048 | tf_op jit(solution)/shard_map/jit(_take)/gather | solution.py:115
  417.1 4.4 select_select_fusion
  421.5 3.0 copy.153
  424.5 69.9 %all_to_all.30 = bf16[16,16,6,1792]{3,0,2,1:T(8,128)(2,1)S(1)} all-to-all(bf16[16,16,6,1792]{3,0,2,1:T(8,128)(2,1)S(1)} %copy.153), channel_id=1, replica_groups=mesh['group'=16,'ingroup'=16] {'group'}, dimensions={1} | all-to-all | bytes 11010048 | tf_op jit(solution)/shard_map/all_to_all | solution.py:120
  494.4 5.4 copy.154
  499.8 6.2 all-to-all-start.5
  506.0 2.3 select_reduce_fusion.2
  508.6 0.3 compare_select_fusion
  508.9 0.2 reshape.278
  509.0 0.2 copy.140
  509.8 0.1 copy.160
  510.2 117.6 %all-to-all-done.5 = bf16[16,16,6,1792]{3,1,2,0:T(8,128)(2,1)} async-done(((bf16[16,16,6,1792]{3,1,2,0:T(8,128)(2,1)}), bf16[16,16,6,1792]{3,1,2,0:T(8,128)(2,1)}, u32[]{:S(2)}, u32[]{:S(2)}) %all-to-all-start.5) | async-done | bytes 5505056 | tf_op jit(solution)/shard_map/all_to_all | solution.py:119
  627.7 7.7 %copy.155 = bf16[16,16,6,1792]{3,2,1,0:T(8,128)(2,1)} copy(bf16[16,16,6,1792]{3,1,2,0:T(8,128)(2,1)} %all-to-all-done.5) | data formatting | bytes 11010048 | tf_op jit(solution)/shard_map/all_to_all | solution.py:119
  635.4 9.7 %reshape.250 = bf16[1536,1792]{1,0:T(8,128)(2,1)} reshape(bf16[16,16,6,1792]{3,2,1,0:T(8,128)(2,1)} %copy.155) | data formatting | bytes 11010048 | tf_op jit(solution)/shard_map/reshape | solution.py:131
  645.1 11.2 %gather_fusion.3 = bf16[1024,1792]{1,0:T(8,128)(2,1)} fusion(bf16[1536,1792]{1,0:T(8,128)(2,1)} %reshape.250, s32[1024]{0:T(1024)S(1)} %broadcast_clamp_fusion), kind=kCustom, calls=%fused_computation.3 | custom fusion | bytes 7344128 | tf_op jit(solution)/shard_map/jit(_take)/gather | solution.py:131
  656.3 8.6 %reshape.277 = bf16[64,8,2,1792]{3,2,1,0:T(2,128)(2,1)} reshape(bf16[1024,1792]{1,0:T(8,128)(2,1)} %gather_fusion.3) | data formatting | bytes 7340032 | tf_op jit(solution)/shard_map/jit(_take)/gather | solution.py:131
  664.9 8.5 %fusion.3 = f32[64,8,2,1792]{3,2,1,0:T(2,128)} fusion(bf16[64,8,2,1792]{3,2,1,0:T(2,128)(2,1)} %reshape.277, pred[64,8,2]{2,1,0:T(8,128)(4,1)S(1)} %copy.140), kind=kLoop, calls=%fused_computation.19 | loop fusion | flops 3670016 | bytes 11011072 | tf_op jit(solution)/shard_map/convert_element_type | solution.py:132
  673.4 10.0 %reshape.251 = f32[64,8,3584]{2,1,0:T(8,128)} reshape(f32[64,8,2,1792]{3,2,1,0:T(2,128)} %fusion.3) | data formatting | bytes 14680064 | tf_op jit(solution)/shard_map/convert_element_type | solution.py:132
  683.4 6.9 broadcast_multiply_fusion
  690.3 16.6 %gather_fusion.4 = f32[512,3584]{1,0:T(8,128)} fusion(f32[64,8,3584]{2,1,0:T(8,128)} %broadcast_multiply_fusion, s32[512]{0:T(512)S(1)} %reshape.284), kind=kCustom, calls=%fused_computation.4 | custom fusion | bytes 14684160 | tf_op jit(solution)/shard_map/jit(take_along_axis)/gather | solution.py:141
  706.9 6.2 fusion.2
  713.1 2.4 convert_reduce_fusion
  715.5 0.8 multiply_convert_fusion.2
  (63 shorter events, 2.6 us)
Async XLA Ops:
  0.0 78.6 %copy-start.1 = (bf16[64,3584]{1,0:T(8,128)(2,1)S(1)}, bf16[64,3584]{1,0:T(8,128)(2,1)}, u32[]{:S(2)}) copy-start(bf16[64,3584]{1,0:T(8,128)(2,1)} %param.7) | copy-start | bytes 1376260
  73.7 31.1 %all-to-all-start = ((s32[16,16,6]{0,2,1:T(8,128)}), s32[16,16,6]{0,2,1:T(8,128)S(1)}, u32[]{:S(2)}, u32[]{:S(2)}) async-start(s32[16,16,6]{0,2,1:T(8,128)} %copy.142), calls=%async_computation | async-start | bytes 131072 | tf_op jit(solution)/shard_map/all_to_all | solution.py:82
  104.8 87.7 %all-to-all-start.2 = ((bf16[16,16,6,1792]{3,0,2,1:T(8,128)(2,1)}), bf16[16,16,6,1792]{3,0,2,1:T(8,128)(2,1)}, u32[]{:S(2)}, u32[]{:S(2)}) async-start(bf16[16,16,6,1792]{3,0,2,1:T(8,128)(2,1)} %copy.150), calls=%async_computation.2 | async-start | bytes 11010048 | tf_op jit(solution)/shard_map/all_to_all | solution.py:75
  192.5 14.2 %all-to-all-start.1 = ((s32[16,16,6]{1,2,0:T(8,128)}), s32[16,16,6]{1,2,0:T(8,128)S(1)}, u32[]{:S(2)}, u32[]{:S(2)}) async-start(s32[16,16,6]{1,2,0:T(8,128)} %copy.143), calls=%async_computation.1 | async-start | bytes 131072 | tf_op jit(solution)/shard_map/all_to_all | solution.py:81
  206.7 129.0 %all-to-all-start.3 = ((bf16[16,16,6,1792]{3,1,2,0:T(8,128)(2,1)}), bf16[16,16,6,1792]{3,1,2,0:T(8,128)(2,1)}, u32[]{:S(2)}, u32[]{:S(2)}) async-start(bf16[16,16,6,1792]{3,1,2,0:T(8,128)(2,1)} %copy.151), calls=%async_computation.3 | async-start | bytes 11010048 | tf_op jit(solution)/shard_map/all_to_all | solution.py:74
  364.2 8.3 %copy-start = (bf16[1024,1792]{1,0:T(8,128)(2,1)S(1)}, bf16[1024,1792]{1,0:T(8,128)(2,1)}, u32[]{:S(2)}) copy-start(bf16[1024,1792]{1,0:T(8,128)(2,1)} %gather_fusion.1) | copy-start | bytes 11010052
  364.2 8.3 %copy-start.3 = (bf16[1,1792,1024]{2,1,0:T(8,128)(2,1)S(1)}, bf16[1,1792,1024]{2,1,0:T(8,128)(2,1)}, u32[]{:S(2)}) copy-start(bf16[1,1792,1024]{2,1,0:T(8,128)(2,1)} %param.9) | copy-start | bytes 11010052
  371.5 7.2 %collective-permute-start = (bf16[1024,1024]{1,0:T(8,128)(2,1)S(1)}, bf16[1024,1024]{1,0:T(8,128)(2,1)}, u32[]{:S(2)}, u32[]{:S(2)}) collective-permute-start(bf16[1024,1024]{1,0:T(8,128)(2,1)S(1)} %fusion.10), channel_id=1, source_target_pairs={{0,1},{1,0},{2,3},{3,2},{4,5},{5,4},{6,7},{7,6},{8,9},{9,8},{10,11... | collective-permute-start | bytes 6291464 | tf_op jit(solution)/shard_map/ppermute | solution.py:10
  378.1 4.7 collective-permute-start.1
  499.8 9.5 %copy-start.2 = (s32[64,8]{0,1:T(8,128)S(1)}, s32[64,8]{0,1:T(8,128)}, u32[]{:S(2)}) copy-start(s32[64,8]{0,1:T(8,128)} %param.12) | copy-start | bytes 6148
  499.8 128.0 %all-to-all-start.5 = ((bf16[16,16,6,1792]{3,1,2,0:T(8,128)(2,1)}), bf16[16,16,6,1792]{3,1,2,0:T(8,128)(2,1)}, u32[]{:S(2)}, u32[]{:S(2)}) async-start(bf16[16,16,6,1792]{3,1,2,0:T(8,128)(2,1)} %copy.154), calls=%async_computation.5 | async-start | bytes 11010048 | tf_op jit(solution)/shard_map/all_to_all | solution.py:119
where the time goes:
time: 726 us; the launch traced here: 717 us
  waiting for transfers between devices  305 us (42%)
  local copies, waits for them, and re-layouts  177 us (24%)
  blocking collectives  137 us (19%)
  other arithmetic  38.8 us (5%)
  starting transfers between devices  31.8 us (4%)
  matrix products  25.6 us (4%)
    all_to_all x1, waiting for transfers between devices, per_device(): lax.all_to_all(lax.all_to_all(back_rows, 'group', split_axis=1, concat_ax...  118 us
    all_to_all x1, waiting for transfers between devices, per_device(): lax.all_to_all(lax.all_to_all(send_rows, 'group', split_axis=1, concat_ax...  104 us
    all_to_all x1, waiting for transfers between devices, per_device(): lax.all_to_all(send_rows, 'group', split_axis=1, concat_axis=1, tiled=True)  80.3 us
    all_to_all x1, blocking collectives, per_device(): lax.all_to_all(back_rows, 'group', split_axis=1, concat_axis=1, tiled=True)  69.9 us
    all_gather x1, blocking collectives, per_device(): piece = lax.all_gather(packed, ('group', 'ingroup'), axis=0, tiled=True)  67 us
    gather x2, local copies, waits for them, and re-layouts, per_device(): jnp.take(expert_out, jnp.clip(flat_rank, 0, capacity - 1), axis=0)  23.4 us
    gather x2, local copies, waits for them, and re-layouts, per_device(): jnp.take(returned.reshape(slot_total, half_width), flat_pick, axis=0)  19.8 us
    gather x3, local copies, waits for them, and re-layouts, per_device(): partner_terms = jnp.take_along_axis(terms, partner[:, :, None], axis=1)  16.8 us
  transfers between devices with their start and end apart: 7, of which 4 were waited for; matrix products, arithmetic and copies ran while one was open for 9% of the time, Pallas kernels for 0%

commit v1 on v0

--- a/solution.py
+++ b/solution.py
@@ -4,6 +4,22 @@
 from jax.sharding import PartitionSpec as P
 
 TOPG = 4
+
+
+def swapped_with_each(shard, axis, split, join):
+    ways, here = (lax.axis_size(axis), lax.axis_index(axis))
+    width = shard.shape[split] // ways
+    shape = list(shard.shape)
+    shape[split] = width
+    height = shape[join]
+    shape[join] = height * ways
+    full = jnp.zeros(shape, shard.dtype)
+    for mask in range(ways):
+        part = lax.dynamic_slice_in_dim(shard, (here ^ mask) * width, width, axis=split)
+        if mask:
+            part = lax.ppermute(part, axis, [(d, d ^ mask) for d in range(ways)])
+        full = lax.dynamic_update_slice_in_dim(full, part, (here ^ mask) * height, axis=join)
+    return full
 
 
 def from_partner(shard, axis, apart):
@@ -117,7 +133,7 @@
     back_rows = back_rows.reshape(members, groups, expert_most, half_width)
     pick_group = expert_ids // per_group
     returned = lax.all_to_all(
-        lax.all_to_all(back_rows, "group", split_axis=1, concat_axis=1, tiled=True),
+        swapped_with_each(back_rows, "group", 1, 1),
         "ingroup",
         split_axis=0,
         concat_axis=0,

time: 726 us -> 786 us (1.083)
  waiting for transfers between devices: 305 us -> 407 us
  blocking collectives: 137 us -> 67 us
  starting transfers between devices: 31.8 us -> 59.7 us
    ppermute x0 -> x15, waiting for transfers between devices: none -> 101 us  [swapped_with_each(): part = lax.ppermute(part, axis, [(d, d ^ mask) for d in range(ways)])]
    all_to_all x1 -> x0, blocking collectives: 69.9 us -> none  [per_device(): lax.all_to_all(back_rows, 'group', split_axis=1, concat_axis=1, tiled=True)]
    ppermute x0 -> x15, starting transfers between devices: none -> 28.4 us  [swapped_with_each(): part = lax.ppermute(part, axis, [(d, d ^ mask) for d in range(ways)])]
  transfers between devices with their start and end apart: 7 -> 22, of which waited for: 4 -> 11; matrix products, arithmetic and copies ran while one was open for 9% -> 8% of each run, Pallas kernels for 0% -> 0%
where the time goes in v1:
time: 786 us; the launch traced here: 777 us
  waiting for transfers between devices  407 us (52%)
  local copies, waits for them, and re-layouts  176 us (22%)
  blocking collectives  67 us (9%)
  starting transfers between devices  59.7 us (8%)
  other arithmetic  38.8 us (5%)
  matrix products  27.5 us (3%)
    all_to_all x1, waiting for transfers between devices, per_device(): lax.all_to_all(swapped_with_each(back_rows, 'group', 1, 1), 'ingroup', sp...  117 us
    all_to_all x1, waiting for transfers between devices, per_device(): lax.all_to_all(lax.all_to_all(send_rows, 'group', split_axis=1, concat_ax...  104 us
    ppermute x15, waiting for transfers between devices, swapped_with_each(): part = lax.ppermute(part, axis, [(d, d ^ mask) for d in range(ways)])  101 us
    all_to_all x1, waiting for transfers between devices, per_device(): lax.all_to_all(send_rows, 'group', split_axis=1, concat_axis=1, tiled=True)  80.3 us
    all_gather x1, blocking collectives, per_device(): piece = lax.all_gather(packed, ('group', 'ingroup'), axis=0, tiled=True)  67 us
    ppermute x15, starting transfers between devices, swapped_with_each(): part = lax.ppermute(part, axis, [(d, d ^ mask) for d in range(ways)])  28.4 us
    gather x2, local copies, waits for them, and re-layouts, per_device(): jnp.take(expert_out, jnp.clip(flat_rank, 0, capacity - 1), axis=0)  23.4 us
    gather x2, local copies, waits for them, and re-layouts, per_device(): jnp.take(returned.reshape(slot_total, half_width), flat_pick, axis=0)  19.7 us
  transfers between devices with their start and end apart: 22, of which 11 were waited for; matrix products, arithmetic and copies ran while one was open for 8% of the time, Pallas kernels for 0%

profile of v1, /device:TPU:1, one launch (start us, length us, event | category | flops | bytes accessed | tf_op | source)
XLA Modules:
  0.0 776.7 jit_solution(5417043176943327743)
XLA Ops:
  0.0 0.8 copy.122
  0.9 0.9 fusion.22
  2.1 67.0 %all-gather.1 = s32[256,1,256]{2,1,0:T(1,128)S(1)} all-gather(s32[1,1,256]{2,1,0:T(1,128)S(1)} %bitcast.53), channel_id=2, replica_groups=mesh['group'=16,'ingroup'=16] {'group','ingroup'}, dimensions={0}, use_global_device_ids=true | all-gather | bytes 263168 | tf_op jit(solution)/shard_map/all_gather | solution.py:60
  69.1 1.7 fusion
  71.6 0.9 fusion.19
  73.6 4.2 all-to-all-start
  78.5 1.2 reshape.248
  79.7 6.7 gather_fusion
  86.5 9.6 %reshape.253 = bf16[16,16,6,1792]{3,2,1,0:T(8,128)(2,1)} reshape(bf16[1536,1792]{1,0:T(8,128)(2,1)} %gather_fusion) | data formatting | bytes 11010048 | tf_op jit(solution)/shard_map/jit(_take)/gather | solution.py:88
  96.2 4.0 broadcast_select_fusion
  100.2 5.5 copy.147
  105.7 6.7 all-to-all-start.2
  112.4 0.7 copy.140
  113.1 80.3 %all-to-all-done.2 = bf16[16,16,6,1792]{3,0,2,1:T(8,128)(2,1)} async-done(((bf16[16,16,6,1792]{3,0,2,1:T(8,128)(2,1)}), bf16[16,16,6,1792]{3,0,2,1:T(8,128)(2,1)}, u32[]{:S(2)}, u32[]{:S(2)}) %all-to-all-start.2) | async-done | bytes 5505056 | tf_op jit(solution)/shard_map/all_to_all | solution.py:91
  193.4 6.5 all-to-all-start.1
  200.0 7.9 %copy.148 = bf16[16,16,6,1792]{3,1,2,0:T(8,128)(2,1)} copy(bf16[16,16,6,1792]{3,0,2,1:T(8,128)(2,1)} %all-to-all-done.2) | data formatting | bytes 11010048 | tf_op jit(solution)/shard_map/all_to_all | solution.py:91
  207.9 7.2 all-to-all-start.3
  215.5 6.2 scatter_custom_fusion.1
  221.7 11.4 %scatter_custom_fusion = pred[1024]{0:T(1024)(128)(4,1)S(1)} fusion(s32[1536]{0:T(1024)S(1)} %get-tuple-element.13, pred[1536]{0:T(1024)(128)(4,1)S(1)} %broadcast.331, pred[]{:T(512)} %constant.163.clone.1), kind=kCustom, calls=%fused_computation.131 | custom fusion | bytes 1025 | tf_op jit(solution)/shard_map/scatter | solution.py:114
  233.1 103.7 %all-to-all-done.3 = bf16[16,16,6,1792]{3,1,2,0:T(8,128)(2,1)} async-done(((bf16[16,16,6,1792]{3,1,2,0:T(8,128)(2,1)}), bf16[16,16,6,1792]{3,1,2,0:T(8,128)(2,1)}, u32[]{:S(2)}, u32[]{:S(2)}) %all-to-all-start.3) | async-done | bytes 5505056 | tf_op jit(solution)/shard_map/all_to_all | solution.py:90
  336.8 7.7 copy.149
  344.5 9.7 %reshape.249 = bf16[1536,1792]{1,0:T(8,128)(2,1)} reshape(bf16[16,16,6,1792]{3,2,1,0:T(8,128)(2,1)} %copy.149) | data formatting | bytes 11010048 | tf_op jit(solution)/shard_map/reshape | solution.py:107
  354.2 11.2 %gather_fusion.1 = bf16[1024,1792]{1,0:T(8,128)(2,1)} fusion(bf16[1536,1792]{1,0:T(8,128)(2,1)} %reshape.249, s32[1024]{0:T(1024)S(1)} %fusion.37), kind=kCustom, calls=%fused_computation.1 | custom fusion | bytes 7344128 | tf_op jit(solution)/shard_map/jit(_take)/gather | solution.py:116
  365.4 8.6 %fusion.10 = bf16[1024,1024]{1,0:T(8,128)(2,1)} fusion(bf16[1,1792,1024]{2,1,0:T(8,128)(2,1)} %param.8, bf16[1024,1792]{1,0:T(8,128)(2,1)} %gather_fusion.1, pred[1024]{0:T(1024)(128)(4,1)S(1)} %compare_and_fusion.3, pred[1024]{0:T(1024)(128)(4,1)S(1)} %scatter_custom_fusion), kind=kOutput, calls=%fused_computation.28 | convolution fusion | flops 3762814976 | bytes 9439232 | tf_op jit(solution)/shard_map/dot_general | solution.py:118
  374.0 0.9 collective-permute-start
  374.9 5.7 fusion.13
  381.3 3.9 collective-permute-done.1
  385.3 11.4 %convolution_convert_fusion = bf16[1024,1792]{1,0:T(8,128)(2,1)} fusion(bf16[1,1024,1792]{2,1,0:T(8,128)(2,1)} %param.10, bf16[1024,1024]{1,0:T(8,128)(2,1)} %collective-permute-done.1, bf16[1024,1024]{1,0:T(8,128)(2,1)} %fusion.13, bf16[1024,1024]{1,0:T(8,128)(2,1)} %collective-permute-done, bf16[1024,1024]{1,0:T(8,128)(2,1)} %fusion.10), kind=kOutput, calls=%fused_computation.18 | convolution fusion | flops 3772514304 | bytes 15728640 | tf_op jit(solution)/shard_map/dot_general | solution.py:128
  396.7 13.9 %gather_fusion.2 = bf16[1536,1792]{1,0:T(8,128)(2,1)} fusion(bf16[1024,1792]{1,0:T(8,128)(2,1)} %convolution_convert_fusion, s32[2048]{0:T(1024)S(1)} %pad_clamp_fusion), kind=kCustom, calls=%fused_computation.2 | custom fusion | bytes 11016192 | tf_op jit(solution)/shard_map/jit(_take)/gather | solution.py:131
  410.6 9.6 %gather.25 = bf16[16,16,6,1792]{3,2,1,0:T(8,128)(2,1)} reshape(bf16[1536,1792]{1,0:T(8,128)(2,1)} %gather_fusion.2) | data formatting | bytes 11010048 | tf_op jit(solution)/shard_map/jit(_take)/gather | solution.py:131
  420.1 4.4 select_select_fusion
  425.2 1.0 constant_dynamic-slice_fusion
  426.3 2.4 collective-permute-start.3
  428.7 1.5 collective-permute-start.4
  430.6 7.7 collective-permute-done.2
  438.3 1.3 collective-permute-start.7
  439.6 9.4 %collective-permute-done.3 = bf16[16,1,6,1792]{3,2,1,0:T(8,128)(2,1)S(1)} collective-permute-done((bf16[16,1,6,1792]{3,2,1,0:T(8,128)(2,1)S(1)}, bf16[16,1,6,1792]{3,2,1,0:T(8,128)(2,1)S(1)}, u32[]{:S(2)}, u32[]{:S(2)}) %collective-permute-start.3) | collective-permute-done | bytes 344096 | tf_op jit(solution)/shard_map/ppermute | solution.py:20
  449.1 1.6 collective-permute-start.8
  451.1 2.7 collective-permute-start.9
  454.0 10.0 %collective-permute-done.6 = bf16[16,1,6,1792]{3,2,1,0:T(8,128)(2,1)S(1)} collective-permute-done((bf16[16,1,6,1792]{3,2,1,0:T(8,128)(2,1)S(1)}, bf16[16,1,6,1792]{3,2,1,0:T(8,128)(2,1)S(1)}, u32[]{:S(2)}, u32[]{:S(2)}) %collective-permute-start.6) | collective-permute-done | bytes 344096 | tf_op jit(solution)/shard_map/ppermute | solution.py:20
  464.0 4.0 collective-permute-start.11
  468.1 7.0 collective-permute-done.7
  475.1 4.2 collective-permute-start.12
  479.3 1.9 collective-permute-start.13
  481.3 36.3 %collective-permute-done.9 = bf16[16,1,6,1792]{3,2,1,0:T(8,128)(2,1)S(1)} collective-permute-done((bf16[16,1,6,1792]{3,2,1,0:T(8,128)(2,1)S(1)}, bf16[16,1,6,1792]{3,2,1,0:T(8,128)(2,1)S(1)}, u32[]{:S(2)}, u32[]{:S(2)}) %collective-permute-start.9) | collective-permute-done | bytes 344096 | tf_op jit(solution)/shard_map/ppermute | solution.py:20
  517.6 2.1 collective-permute-start.14
  519.8 4.7 collective-permute-start.15
  524.6 1.4 collective-permute-start.16
  526.1 30.7 %collective-permute-done.13 = bf16[16,1,6,1792]{3,2,1,0:T(8,128)(2,1)S(1)} collective-permute-done((bf16[16,1,6,1792]{3,2,1,0:T(8,128)(2,1)S(1)}, bf16[16,1,6,1792]{3,2,1,0:T(8,128)(2,1)S(1)}, u32[]{:S(2)}, u32[]{:S(2)}) %collective-permute-start.13) | collective-permute-done | bytes 344096 | tf_op jit(solution)/shard_map/ppermute | solution.py:20
  557.2 3.7 copy.150
  560.9 5.5 all-to-all-start.4
  566.4 2.3 select_reduce_fusion.2
  570.5 117.4 %all-to-all-done.4 = bf16[16,16,6,1792]{3,1,2,0:T(8,128)(2,1)} async-done(((bf16[16,16,6,1792]{3,1,2,0:T(8,128)(2,1)}), bf16[16,16,6,1792]{3,1,2,0:T(8,128)(2,1)}, u32[]{:S(2)}, u32[]{:S(2)}) %all-to-all-start.4) | async-done | bytes 5505056 | tf_op jit(solution)/shard_map/all_to_all | solution.py:135
  688.0 7.7 copy.151
  695.7 9.7 %reshape.250 = bf16[1536,1792]{1,0:T(8,128)(2,1)} reshape(bf16[16,16,6,1792]{3,2,1,0:T(8,128)(2,1)} %copy.151) | data formatting | bytes 11010048 | tf_op jit(solution)/shard_map/reshape | solution.py:147
  705.3 11.2 %gather_fusion.3 = bf16[1024,1792]{1,0:T(8,128)(2,1)} fusion(bf16[1536,1792]{1,0:T(8,128)(2,1)} %reshape.250, s32[1024]{0:T(1024)S(1)} %broadcast_clamp_fusion), kind=kCustom, calls=%fused_computation.3 | custom fusion | bytes 7344128 | tf_op jit(solution)/shard_map/jit(_take)/gather | solution.py:147
  716.5 8.5 %reshape.277 = bf16[64,8,2,1792]{3,2,1,0:T(2,128)(2,1)} reshape(bf16[1024,1792]{1,0:T(8,128)(2,1)} %gather_fusion.3) | data formatting | bytes 7340032 | tf_op jit(solution)/shard_map/jit(_take)/gather | solution.py:147
  725.0 8.5 %fusion.3 = f32[64,8,2,1792]{3,2,1,0:T(2,128)} fusion(bf16[64,8,2,1792]{3,2,1,0:T(2,128)(2,1)} %reshape.277, pred[64,8,2]{2,1,0:T(8,128)(4,1)S(1)} %copy.137), kind=kLoop, calls=%fused_computation.19 | loop fusion | flops 3670016 | bytes 11011072 | tf_op jit(solution)/shard_map/convert_element_type | solution.py:148
  733.6 10.0 %reshape.251 = f32[64,8,3584]{2,1,0:T(8,128)} reshape(f32[64,8,2,1792]{3,2,1,0:T(2,128)} %fusion.3) | data formatting | bytes 14680064 | tf_op jit(solution)/shard_map/convert_element_type | solution.py:148
  743.6 6.9 broadcast_multiply_fusion
  750.4 16.6 %gather_fusion.4 = f32[512,3584]{1,0:T(8,128)} fusion(f32[64,8,3584]{2,1,0:T(8,128)} %broadcast_multiply_fusion, s32[512]{0:T(512)S(1)} %reshape.284), kind=kCustom, calls=%fused_computation.4 | custom fusion | bytes 14684160 | tf_op jit(solution)/shard_map/jit(take_along_axis)/gather | solution.py:157
  767.1 6.2 fusion.2
  773.2 2.4 convert_reduce_fusion
  775.7 0.8 multiply_convert_fusion.2
  (106 shorter events, 8.4 us)
Async XLA Ops:
  73.6 32.1 %all-to-all-start = ((s32[16,16,6]{0,2,1:T(8,128)}), s32[16,16,6]{0,2,1:T(8,128)S(1)}, u32[]{:S(2)}, u32[]{:S(2)}) async-start(s32[16,16,6]{0,2,1:T(8,128)} %copy.139), calls=%async_computation | async-start | bytes 131072 | tf_op jit(solution)/shard_map/all_to_all | solution.py:98
  105.7 87.7 %all-to-all-start.2 = ((bf16[16,16,6,1792]{3,0,2,1:T(8,128)(2,1)}), bf16[16,16,6,1792]{3,0,2,1:T(8,128)(2,1)}, u32[]{:S(2)}, u32[]{:S(2)}) async-start(bf16[16,16,6,1792]{3,0,2,1:T(8,128)(2,1)} %copy.147), calls=%async_computation.2 | async-start | bytes 11010048 | tf_op jit(solution)/shard_map/all_to_all | solution.py:91
  193.4 14.4 %all-to-all-start.1 = ((s32[16,16,6]{1,2,0:T(8,128)}), s32[16,16,6]{1,2,0:T(8,128)S(1)}, u32[]{:S(2)}, u32[]{:S(2)}) async-start(s32[16,16,6]{1,2,0:T(8,128)} %copy.140), calls=%async_computation.1 | async-start | bytes 131072 | tf_op jit(solution)/shard_map/all_to_all | solution.py:97
  207.9 129.0 %all-to-all-start.3 = ((bf16[16,16,6,1792]{3,1,2,0:T(8,128)(2,1)}), bf16[16,16,6,1792]{3,1,2,0:T(8,128)(2,1)}, u32[]{:S(2)}, u32[]{:S(2)}) async-start(bf16[16,16,6,1792]{3,1,2,0:T(8,128)(2,1)} %copy.148), calls=%async_computation.3 | async-start | bytes 11010048 | tf_op jit(solution)/shard_map/all_to_all | solution.py:90
  365.4 9.5 %copy-start = (bf16[1024,1792]{1,0:T(8,128)(2,1)S(1)}, bf16[1024,1792]{1,0:T(8,128)(2,1)}, u32[]{:S(2)}) copy-start(bf16[1024,1792]{1,0:T(8,128)(2,1)} %gather_fusion.1) | copy-start | bytes 11010052
  365.4 9.5 %copy-start.2 = (bf16[1,1792,1024]{2,1,0:T(8,128)(2,1)S(1)}, bf16[1,1792,1024]{2,1,0:T(8,128)(2,1)}, u32[]{:S(2)}) copy-start(bf16[1,1792,1024]{2,1,0:T(8,128)(2,1)} %param.9) | copy-start | bytes 11010052
  374.0 7.3 collective-permute-start
  380.6 4.7 collective-permute-start.1
  426.2 12.1 %collective-permute-start.2 = (bf16[16,1,6,1792]{3,2,1,0:T(8,128)(2,1)S(1)}, bf16[16,1,6,1792]{3,2,1,0:T(8,128)(2,1)S(1)}, u32[]{:S(2)}, u32[]{:S(2)}) collective-permute-start(bf16[16,1,6,1792]{3,2,1,0:T(8,128)(2,1)S(1)} %get-tuple-element.28), channel_id=1, source_target_pairs={{0,16},{16,0},{32,48},{48,32},{64,80},{80,64},{96,112},{112,96},{1... | collective-permute-start | bytes 1032200 | tf_op jit(solution)/shard_map/ppermute | solution.py:20
  426.3 22.7 %collective-permute-start.3 = (bf16[16,1,6,1792]{3,2,1,0:T(8,128)(2,1)S(1)}, bf16[16,1,6,1792]{3,2,1,0:T(8,128)(2,1)S(1)}, u32[]{:S(2)}, u32[]{:S(2)}) collective-permute-start(bf16[16,1,6,1792]{3,2,1,0:T(8,128)(2,1)S(1)} %get-tuple-element.27), channel_id=1, source_target_pairs={{0,32},{16,48},{32,0},{48,16},{64,96},{80,112},{96,64},{112,80},{1... | collective-permute-start | bytes 1032200 | tf_op jit(solution)/shard_map/ppermute | solution.py:20
  428.7 22.4 %collective-permute-start.4 = (bf16[16,1,6,1792]{3,2,1,0:T(8,128)(2,1)S(1)}, bf16[16,1,6,1792]{3,2,1,0:T(8,128)(2,1)S(1)}, u32[]{:S(2)}, u32[]{:S(2)}) collective-permute-start(bf16[16,1,6,1792]{3,2,1,0:T(8,128)(2,1)S(1)} %get-tuple-element.26), channel_id=1, source_target_pairs={{0,48},{16,32},{32,16},{48,0},{64,112},{80,96},{96,80},{112,64},{1... | collective-permute-start | bytes 1032200 | tf_op jit(solution)/shard_map/ppermute | solution.py:20
  430.2 23.7 %collective-permute-start.5 = (bf16[16,1,6,1792]{3,2,1,0:T(8,128)(2,1)S(1)}, bf16[16,1,6,1792]{3,2,1,0:T(8,128)(2,1)S(1)}, u32[]{:S(2)}, u32[]{:S(2)}) collective-permute-start(bf16[16,1,6,1792]{3,2,1,0:T(8,128)(2,1)S(1)} %get-tuple-element.25), channel_id=1, source_target_pairs={{0,64},{16,80},{32,96},{48,112},{64,0},{80,16},{96,32},{112,48},{1... | collective-permute-start | bytes 1032200 | tf_op jit(solution)/shard_map/ppermute | solution.py:20
  430.6 33.5 %collective-permute-start.6 = (bf16[16,1,6,1792]{3,2,1,0:T(8,128)(2,1)S(1)}, bf16[16,1,6,1792]{3,2,1,0:T(8,128)(2,1)S(1)}, u32[]{:S(2)}, u32[]{:S(2)}) collective-permute-start(bf16[16,1,6,1792]{3,2,1,0:T(8,128)(2,1)S(1)} %get-tuple-element.24), channel_id=1, source_target_pairs={{0,80},{16,64},{32,112},{48,96},{64,16},{80,0},{96,48},{112,32},{1... | collective-permute-start | bytes 1032200 | tf_op jit(solution)/shard_map/ppermute | solution.py:20
  438.3 36.8 %collective-permute-start.7 = (bf16[16,1,6,1792]{3,2,1,0:T(8,128)(2,1)S(1)}, bf16[16,1,6,1792]{3,2,1,0:T(8,128)(2,1)S(1)}, u32[]{:S(2)}, u32[]{:S(2)}) collective-permute-start(bf16[16,1,6,1792]{3,2,1,0:T(8,128)(2,1)S(1)} %get-tuple-element.23), channel_id=1, source_target_pairs={{0,96},{16,112},{32,64},{48,80},{64,32},{80,48},{96,0},{112,16},{1... | collective-permute-start | bytes 1032200 | tf_op jit(solution)/shard_map/ppermute | solution.py:20
  449.1 30.2 %collective-permute-start.8 = (bf16[16,1,6,1792]{3,2,1,0:T(8,128)(2,1)S(1)}, bf16[16,1,6,1792]{3,2,1,0:T(8,128)(2,1)S(1)}, u32[]{:S(2)}, u32[]{:S(2)}) collective-permute-start(bf16[16,1,6,1792]{3,2,1,0:T(8,128)(2,1)S(1)} %get-tuple-element.22), channel_id=1, source_target_pairs={{0,112},{16,96},{32,80},{48,64},{64,48},{80,32},{96,16},{112,0},{1... | collective-permute-start | bytes 1032200 | tf_op jit(solution)/shard_map/ppermute | solution.py:20
  451.1 66.5 %collective-permute-start.9 = (bf16[16,1,6,1792]{3,2,1,0:T(8,128)(2,1)S(1)}, bf16[16,1,6,1792]{3,2,1,0:T(8,128)(2,1)S(1)}, u32[]{:S(2)}, u32[]{:S(2)}) collective-permute-start(bf16[16,1,6,1792]{3,2,1,0:T(8,128)(2,1)S(1)} %get-tuple-element.21), channel_id=1, source_target_pairs={{0,128},{16,144},{32,160},{48,176},{64,192},{80,208},{96,224},{112... | collective-permute-start | bytes 1032200 | tf_op jit(solution)/shard_map/ppermute | solution.py:20
  453.9 65.9 %collective-permute-start.10 = (bf16[16,1,6,1792]{3,2,1,0:T(8,128)(2,1)S(1)}, bf16[16,1,6,1792]{3,2,1,0:T(8,128)(2,1)S(1)}, u32[]{:S(2)}, u32[]{:S(2)}) collective-permute-start(bf16[16,1,6,1792]{3,2,1,0:T(8,128)(2,1)S(1)} %get-tuple-element.20), channel_id=1, source_target_pairs={{0,144},{16,128},{32,176},{48,160},{64,208},{80,192},{96,240},{112... | collective-permute-start | bytes 1032200 | tf_op jit(solution)/shard_map/ppermute | solution.py:20
  464.0 60.6 %collective-permute-start.11 = (bf16[16,1,6,1792]{3,2,1,0:T(8,128)(2,1)S(1)}, bf16[16,1,6,1792]{3,2,1,0:T(8,128)(2,1)S(1)}, u32[]{:S(2)}, u32[]{:S(2)}) collective-permute-start(bf16[16,1,6,1792]{3,2,1,0:T(8,128)(2,1)S(1)} %get-tuple-element.19), channel_id=1, source_target_pairs={{0,160},{16,176},{32,128},{48,144},{64,224},{80,240},{96,192},{112... | collective-permute-start | bytes 1032200 | tf_op jit(solution)/shard_map/ppermute | solution.py:20
  475.1 51.0 %collective-permute-start.12 = (bf16[16,1,6,1792]{3,2,1,0:T(8,128)(2,1)S(1)}, bf16[16,1,6,1792]{3,2,1,0:T(8,128)(2,1)S(1)}, u32[]{:S(2)}, u32[]{:S(2)}) collective-permute-start(bf16[16,1,6,1792]{3,2,1,0:T(8,128)(2,1)S(1)} %get-tuple-element.18), channel_id=1, source_target_pairs={{0,176},{16,160},{32,144},{48,128},{64,240},{80,224},{96,208},{112... | collective-permute-start | bytes 1032200 | tf_op jit(solution)/shard_map/ppermute | solution.py:20
  479.3 77.6 %collective-permute-start.13 = (bf16[16,1,6,1792]{3,2,1,0:T(8,128)(2,1)S(1)}, bf16[16,1,6,1792]{3,2,1,0:T(8,128)(2,1)S(1)}, u32[]{:S(2)}, u32[]{:S(2)}) collective-permute-start(bf16[16,1,6,1792]{3,2,1,0:T(8,128)(2,1)S(1)} %get-tuple-element.17), channel_id=1, source_target_pairs={{0,192},{16,208},{32,224},{48,240},{64,128},{80,144},{96,160},{112... | collective-permute-start | bytes 1032200 | tf_op jit(solution)/shard_map/ppermute | solution.py:20
  517.6 39.3 %collective-permute-start.14 = (bf16[16,1,6,1792]{3,2,1,0:T(8,128)(2,1)S(1)}, bf16[16,1,6,1792]{3,2,1,0:T(8,128)(2,1)S(1)}, u32[]{:S(2)}, u32[]{:S(2)}) collective-permute-start(bf16[16,1,6,1792]{3,2,1,0:T(8,128)(2,1)S(1)} %get-tuple-element.16), channel_id=1, source_target_pairs={{0,208},{16,192},{32,240},{48,224},{64,144},{80,128},{96,176},{112... | collective-permute-start | bytes 1032200 | tf_op jit(solution)/shard_map/ppermute | solution.py:20
  519.8 37.2 %collective-permute-start.15 = (bf16[16,1,6,1792]{3,2,1,0:T(8,128)(2,1)S(1)}, bf16[16,1,6,1792]{3,2,1,0:T(8,128)(2,1)S(1)}, u32[]{:S(2)}, u32[]{:S(2)}) collective-permute-start(bf16[16,1,6,1792]{3,2,1,0:T(8,128)(2,1)S(1)} %get-tuple-element.15), channel_id=1, source_target_pairs={{0,224},{16,240},{32,192},{48,208},{64,160},{80,176},{96,128},{112... | collective-permute-start | bytes 1032200 | tf_op jit(solution)/shard_map/ppermute | solution.py:20
  524.6 32.5 %collective-permute-start.16 = (bf16[16,1,6,1792]{3,2,1,0:T(8,128)(2,1)S(1)}, bf16[16,1,6,1792]{3,2,1,0:T(8,128)(2,1)S(1)}, u32[]{:S(2)}, u32[]{:S(2)}) collective-permute-start(bf16[16,1,6,1792]{3,2,1,0:T(8,128)(2,1)S(1)} %get-tuple-element.14), channel_id=1, source_target_pairs={{0,240},{16,224},{32,208},{48,192},{64,176},{80,160},{96,144},{112... | collective-permute-start | bytes 1032200 | tf_op jit(solution)/shard_map/ppermute | solution.py:20
  560.9 8.8 %copy-start.1 = (s32[64,8]{0,1:T(8,128)S(1)}, s32[64,8]{0,1:T(8,128)}, u32[]{:S(2)}) copy-start(s32[64,8]{0,1:T(8,128)} %param.12) | copy-start | bytes 6148
  560.9 127.1 %all-to-all-start.4 = ((bf16[16,16,6,1792]{3,1,2,0:T(8,128)(2,1)}), bf16[16,16,6,1792]{3,1,2,0:T(8,128)(2,1)}, u32[]{:S(2)}, u32[]{:S(2)}) async-start(bf16[16,16,6,1792]{3,1,2,0:T(8,128)(2,1)} %copy.150), calls=%async_computation.4 | async-start | bytes 11010048 | tf_op jit(solution)/shard_map/all_to_all | solution.py:135
